TPU v7x, 32 devices: a whole 2x2x4 slice. The times are simulated.
32 devices in a mesh: head: 4 (over y, core), tok: 8 (over z, x).
Axes of the slice: x: 2, y: 2, z: 4, core: 2. Of those that a mesh axis runs over, the one named last changes fastest.
Arguments:
- hires_tokens: bfloat16 [32768, 1024], P('tok'), may hold values from -6 to 6
- lowres_tokens: bfloat16 [2048, 1024], P('tok'), may hold values from -6 to 6
- norm_gain: float32 [1024], replicated, may hold values from 0.1 to 1.9
- w_cross_q: bfloat16 [1024, 1024], P(None, 'head'), may hold values from -0.1875 to 0.1875
- w_low_kv: bfloat16 [1024, 2, 1024], P(None, None, 'head'), may hold values from -0.1875 to 0.1875
- w_view_qkv: bfloat16 [1024, 3, 1024], P(None, None, 'head'), may hold values from -0.1875 to 0.1875
- w_out: bfloat16 [2, 1024, 1024], P(None, 'head'), may hold values from -0.125 to 0.125
- block_lists: int32 [256, 8], P('tok'), may hold values from 0 to 15, as said below
- block_counts: int32 [256], P('tok'), may hold values from 1 to 8, as said below
Outputs:
- layer_out: bfloat16 [32768, 1024], P('tok', 'head')
Inputs may be any that keep to these rules, and one draw needn't show every extreme that they name: `block_lists`: each row names 8 distinct low-resolution blocks; only the first block_counts entries of a row are used. `block_counts`: in every draw there is at least one index of tok all of whose query blocks use all 8 entries; query blocks of the other indices may use any count from 1 to 8.
All inputs are finite; a program needn't handle non-finite values.
Results may differ from a plain program's by a relative error of at most 0.009.
Values may be sent and summed in bfloat16 or wider, within the bound.
No kernel may reach another device: no remote copies, remote signals or barrier semaphores. Data moves between devices by JAX's collectives and lax.ppermute only.
A program may use at most 128 MiB of HBM per device.

v0:
```python
import math

import jax
import jax.numpy as jnp
from jax import lax
from jax.sharding import PartitionSpec as P

HD = 128
VIEWS = 8
BLOCK = 128
MAXB = 8


def rms_rows(row_block, norm_gain):
    values = row_block.astype(jnp.float32)
    factor = lax.rsqrt(jnp.mean(values * values, axis=-1, keepdims=True) + 1e-06)
    return (values * factor * norm_gain).astype(jnp.bfloat16)


def masked_softmax(scores, is_valid):
    exponent = jnp.where(is_valid, jnp.exp(scores), jnp.zeros_like(scores))
    return (exponent / jnp.sum(exponent, axis=-1, keepdims=True)).astype(jnp.bfloat16)


def shards(
    hires_tokens,
    lowres_tokens,
    norm_gain,
    w_cross_q,
    w_low_kv,
    w_view_qkv,
    w_out,
    block_lists,
    block_counts,
):
    tok_rows, model_width = hires_tokens.shape
    local_cols = w_cross_q.shape[1]
    heads_here = local_cols // HD
    normed = rms_rows(hires_tokens, norm_gain)
    low_normed = rms_rows(lowres_tokens, norm_gain)
    cross_query = jnp.dot(normed, w_cross_q, preferred_element_type=jnp.float32).astype(
        jnp.bfloat16
    )
    low_kv = jnp.dot(
        low_normed,
        w_low_kv.reshape(model_width, 2 * local_cols),
        preferred_element_type=jnp.float32,
    ).astype(jnp.bfloat16)
    all_kv = lax.all_gather(low_kv, "tok", axis=0, tiled=True)
    low_blocks = all_kv.reshape(-1, BLOCK, 2, heads_here, HD)
    q_blocks = tok_rows // BLOCK
    group_size = math.gcd(q_blocks, max(1, 512 // BLOCK))
    grouped_q = cross_query.reshape(q_blocks // group_size, group_size, BLOCK, heads_here, HD)
    grouped_ids = block_lists.reshape(q_blocks // group_size, group_size, MAXB)
    grouped_counts = block_counts.reshape(q_blocks // group_size, group_size)
    slot_of_key = jnp.arange(MAXB * BLOCK, dtype=jnp.int32) // BLOCK

    def attend_group(inputs):
        queries, block_ids, counts = inputs
        picked = low_blocks[block_ids].reshape(group_size, MAXB * BLOCK, 2, heads_here, HD)
        scores = jnp.einsum(
            "gqhe,gkhe->ghqk", queries, picked[:, :, 0], preferred_element_type=jnp.float32
        ) / math.sqrt(HD)
        is_valid = (slot_of_key[None, :] < counts[:, None])[:, None, None, :]
        weights = masked_softmax(scores, is_valid)
        mixed_out = jnp.einsum(
            "ghqk,gkhe->gqhe", weights, picked[:, :, 1], preferred_element_type=jnp.float32
        )
        return mixed_out.astype(jnp.bfloat16)

    cross_out = lax.map(attend_group, (grouped_q, grouped_ids, grouped_counts)).reshape(
        tok_rows, local_cols
    )
    view_qkv = jnp.dot(
        normed, w_view_qkv.reshape(model_width, 3 * local_cols), preferred_element_type=jnp.float32
    )
    view_qkv = view_qkv.astype(jnp.bfloat16).reshape(tok_rows, 3, local_cols)
    arrived = lax.all_to_all(view_qkv, "tok", split_axis=0, concat_axis=0, tiled=True)
    per_view = arrived.reshape(VIEWS, -1, 3, heads_here, HD)
    scores = jnp.einsum(
        "vphe,uphe->phvu", per_view[:, :, 0], per_view[:, :, 1], preferred_element_type=jnp.float32
    ) / math.sqrt(HD)
    weights = masked_softmax(scores, True)
    mixed_out = jnp.einsum(
        "phvu,uphe->vphe", weights, per_view[:, :, 2], preferred_element_type=jnp.float32
    )
    view_out = lax.all_to_all(
        mixed_out.astype(jnp.bfloat16).reshape(tok_rows, local_cols),
        "tok",
        split_axis=0,
        concat_axis=0,
        tiled=True,
    )
    partial_value = jnp.dot(cross_out, w_out[0], preferred_element_type=jnp.float32)
    partial_value = partial_value + jnp.dot(view_out, w_out[1], preferred_element_type=jnp.float32)
    summed = lax.psum_scatter(
        partial_value.astype(jnp.bfloat16), "head", scatter_dimension=1, tiled=True
    ).astype(jnp.float32)
    out_cols = summed.shape[1]
    residual = lax.dynamic_slice_in_dim(
        hires_tokens, lax.axis_index("head") * out_cols, out_cols, 1
    )
    return (residual.astype(jnp.float32) + summed).astype(jnp.bfloat16)


def solution(mesh):
    in_specs = (
        P("tok", None),
        P("tok", None),
        P(),
        P(None, "head"),
        P(None, None, "head"),
        P(None, None, "head"),
        P(None, "head", None),
        P("tok", None),
        P("tok"),
    )
    out_specs = P("tok", "head")
    return jax.shard_map(shards, mesh=mesh, in_specs=in_specs, out_specs=out_specs, check_vma=False)
```

profile of v0, /device:TPU:0, one launch (start us, length us, event | category | flops | bytes accessed | tf_op | source)
XLA Modules:
  0.0 577.5 jit_solution(14619641682360562503)
XLA Ops:
  6.5 5.2 fusion.19
  13.6 11.4 %convolution_convert_fusion = bf16[4096,768]{0,1:T(8,128)(2,1)} fusion(bf16[1024,768]{0,1:T(8,128)(2,1)} %bitcast.83, bf16[4096,1024]{1,0:T(8,128)(2,1)} %param.11, f32[1024]{0:T(1024)S(1)} %copy-done.7, f32[4096]{0:T(1024)S(1)} %add_rsqrt_fusion), kind=kOutput, calls=%fused_computation.35 | convolution fusion | flops 6462373888 | bytes 16273408 | tf_op jit(solution)/shard_map/dot_general | solution.py:74
  25.0 13.1 %copy.63 = bf16[4096,3,256]{2,1,0:T(4,128)(2,1)} copy(bf16[4096,3,256]{0,2,1:T(8,128)(2,1)} %bitcast.81) | data formatting | bytes 12582912 | tf_op jit(solution)/shard_map/reshape | solution.py:77
  38.1 7.4 %all-to-all-start = ((bf16[4096,3,256]{2,1,0:T(4,128)(2,1)}), bf16[4096,3,256]{2,1,0:T(4,128)(2,1)}, u32[]{:S(2)}, u32[]{:S(2)}) async-start(bf16[4096,3,256]{2,1,0:T(4,128)(2,1)} %copy.63), calls=%async_computation | async-start | bytes 16777216 | tf_op jit(solution)/shard_map/all_to_all | solution.py:78
  47.9 6.1 %convolution_convert_fusion.1 = bf16[4096,256]{1,0:T(8,128)(2,1)S(1)} fusion(bf16[1024,256]{1,0:T(8,128)(2,1)S(1)} %copy-done, bf16[4096,1024]{1,0:T(8,128)(2,1)} %param.11, f32[1024]{0:T(1024)S(1)} %copy-done.7, f32[4096]{0:T(1024)S(1)} %add_rsqrt_fusion), kind=kOutput, calls=%fused_computation.36 | convolution fusion | flops 2165309440 | bytes 11030528 | tf_op jit(solution)/shard_map/dot_general | solution.py:41
  56.3 162.7 %all-gather.2.cloned.1.call-done = bf16[2048,512]{1,0:T(8,128)(2,1)} async-done(((bf16[256,512]{1,0:T(8,128)(2,1)}), bf16[2048,512]{1,0:T(8,128)(2,1)}) %all-gather.2.cloned.1.call-update) | async-done | bytes 2097168 | tf_op jit(solution)/shard_map/all_gather | solution.py:49
  219.0 4.0 reshape.110
  225.1 28.8 %all-to-all-done = bf16[4096,3,256]{2,1,0:T(4,128)(2,1)} async-done(((bf16[4096,3,256]{2,1,0:T(4,128)(2,1)}), bf16[4096,3,256]{2,1,0:T(4,128)(2,1)}, u32[]{:S(2)}, u32[]{:S(2)}) %all-to-all-start) | async-done | bytes 6291488 | tf_op jit(solution)/shard_map/all_to_all | solution.py:78
  253.9 18.6 %reshape.131 = bf16[8,512,3,2,128]{4,3,2,1,0:T(2,128)(2,1)} reshape(bf16[4096,3,256]{2,1,0:T(4,128)(2,1)} %all-to-all-done) | data formatting | bytes 12582912 | tf_op jit(solution)/shard_map/reshape | solution.py:79
  272.5 7.1 %fusion.41 = (bf16[8,512,1,2,128]{4,3,2,1,0:T(2,128)(2,1)}, bf16[8,512,1,2,128]{4,3,2,1,0:T(2,128)(2,1)S(1)}, bf16[8,512,1,2,128]{4,3,2,1,0:T(2,128)(2,1)S(1)}) fusion(bf16[8,512,3,2,128]{4,3,2,1,0:T(2,128)(2,1)} %reshape.131), kind=kLoop, calls=%fused_computation.65 | loop fusion | bytes 12582912 | tf_op jit(solution)/shard_map/slice | solution.py:85
  279.6 4.5 fusion.27
  289.8 5.2 convert_bitcast_fusion
  295.0 4.4 copy.70
  299.4 4.6 all-to-all-start.1
  304.0 165.2 %while.11 = (s32[]{:T(128)}, bf16[8,4,128,2,128]{4,3,2,1,0:T(2,128)(2,1)}, s32[8,4,8]{2,1,0:T(4,128)S(1)}, bf16[16,128,2,2,128]{4,1,3,2,0:T(8,128)(2,1)S(1)}, s3...) while((s32[]{:T(128)}, bf16[8,4,128,2,128]{4,3,2,1,0:T(2,128)(2,1)}, ...), condition=%wide.region_4.5_spmd.clone, body=%wide.region_2.4_spmd.clone.sunk | while | flops 544354432 | bytes 44074376 | solution.py:71
  304.1 3.0 gather_fusion
  312.5 3.0 fusion.55
  315.6 4.0 copy.114
  319.6 4.1 fusion.56
  324.8 3.0 gather_fusion
  333.2 3.0 fusion.55
  336.2 4.0 copy.114
  340.2 4.1 fusion.56
  345.4 3.0 gather_fusion
  353.8 3.0 fusion.55
  356.9 4.0 copy.114
  360.9 4.1 fusion.56
  366.1 3.0 gather_fusion
  374.5 3.0 fusion.55
  377.5 4.0 copy.114
  381.5 4.1 fusion.56
  386.7 3.0 gather_fusion
  395.1 3.0 fusion.55
  398.2 4.0 copy.114
  402.1 4.1 fusion.56
  415.8 3.0 fusion.55
  418.8 4.0 copy.114
  422.8 4.1 fusion.56
  436.4 3.0 fusion.55
  439.5 4.0 copy.114
  443.4 4.1 fusion.56
  457.1 3.0 fusion.55
  460.1 4.0 copy.114
  464.1 4.1 fusion.56
  469.2 9.7 %fusion.24 = f32[4096,1024]{1,0:T(8,128)} fusion(bf16[512,8,2,128]{3,2,1,0:T(2,128)(2,1)} %bitcast.82, bf16[2,256,1024]{2,1,0:T(8,128)(2,1)} %param.17), kind=kOutput, calls=%fused_computation.38 | convolution fusion | flops 2147483648 | bytes 19398656 | tf_op jit(solution)/shard_map/dot_general | solution.py:94
  481.8 11.5 %add_convert_fusion = bf16[4096,1024]{1,0:T(8,128)(2,1)} fusion(f32[4096,1024]{1,0:T(8,128)} %fusion.24, bf16[4096,256]{1,0:T(8,128)(2,1)S(1)} %bitcast.80, bf16[2,256,1024]{2,1,0:T(8,128)(2,1)} %param.17), kind=kOutput, calls=%fused_computation.34 | convolution fusion | flops 2155872256 | bytes 27787264 | tf_op jit(solution)/shard_map/dot_general | solution.py:95
  493.4 73.1 %reduce-scatter.2.cloned.1.call-done = bf16[4096,256]{1,0:T(8,128)(2,1)} async-done(((bf16[4096,1024]{1,0:T(8,128)(2,1)}), bf16[4096,256]{1,0:T(8,128)(2,1)}) %reduce-scatter.2.cloned.1.call-update) | async-done | bytes 2097168 | tf_op jit(solution)/shard_map/reduce_scatter | solution.py:96
  566.6 4.1 add_convert_fusion.1
  (128 shorter events, 78.4 us)
Async XLA Ops:
  6.5 41.4 %copy-start = (bf16[1024,256]{1,0:T(8,128)(2,1)S(1)}, bf16[1024,256]{1,0:T(8,128)(2,1)}, u32[]{:S(2)}) copy-start(bf16[1024,256]{1,0:T(8,128)(2,1)} %param.14) | copy-start | bytes 1572868
  6.5 5.3 copy-start.2
  11.8 1.8 copy-start.7
  38.1 7.6 %copy-start.3 = (bf16[1024,2,256]{2,1,0:T(2,128)(2,1)S(1)}, bf16[1024,2,256]{2,1,0:T(2,128)(2,1)}, u32[]{:S(2)}) copy-start(bf16[1024,2,256]{2,1,0:T(2,128)(2,1)} %param.15) | copy-start | bytes 3145732
  38.1 215.8 %all-to-all-start = ((bf16[4096,3,256]{2,1,0:T(4,128)(2,1)}), bf16[4096,3,256]{2,1,0:T(4,128)(2,1)}, u32[]{:S(2)}, u32[]{:S(2)}) async-start(bf16[4096,3,256]{2,1,0:T(4,128)(2,1)} %copy.63), calls=%async_computation | async-start | bytes 16777216 | tf_op jit(solution)/shard_map/all_to_all | solution.py:78
  45.5 1.0 copy-start.4
  45.5 173.5 %all-gather.2.cloned.1.call-start = ((), (), s32[]{:S(2)}) async-start(), calls=%async_computation.3 | async-start | bytes 2359296 | tf_op jit(solution)/shard_map/all_gather | solution.py:49
  54.0 2.1 copy-start.5
  54.0 2.2 copy-start.6
  299.4 179.6 %all-to-all-start.1 = ((bf16[8,512,256]{1,2,0:T(8,128)(2,1)}), bf16[8,512,256]{1,2,0:T(8,128)(2,1)}, u32[]{:S(2)}, u32[]{:S(2)}) async-start(bf16[8,512,256]{1,2,0:T(8,128)(2,1)} %bitcast.79), calls=%async_computation.1 | async-start | bytes 4194304 | tf_op jit(solution)/shard_map/all_to_all | solution.py:87
  304.0 262.6 %reduce-scatter.2.cloned.1.call-start = ((), (), s32[]{:S(2)}) async-start(), calls=%async_computation.4 | async-start | bytes 10485760 | tf_op jit(solution)/shard_map/reduce_scatter | solution.py:96
  493.4 77.2 %copy-start.1 = (bf16[1024,256]{1,0:T(8,128)(2,1)S(1)}, bf16[1024,256]{1,0:T(8,128)(2,1)}, u32[]{:S(2)}) copy-start(bf16[1024,256]{1,0:T(8,128)(2,1)} %param.14) | copy-start | bytes 1572868
Sparse Core Ops, SparseCore 0:
  48.4 170.5 all-gather.1
  493.5 72.9 reduce-scatter.1
where the time goes:
time: 580 us; the launch traced here: 577 us
  waiting for transfers between devices  265 us (46%)
  local copies, waits for them, and re-layouts  170 us (29%)
  matrix products  106 us (18%)
  between operations  13.6 us (2%)
  starting transfers between devices  12.2 us (2%)
  other arithmetic  10.4 us (2%)
    all_gather x1, waiting for transfers between devices, shards(): all_kv = lax.all_gather(low_kv, 'tok', axis=0, tiled=True)  163 us
    reduce_scatter x1, waiting for transfers between devices, shards(): lax.psum_scatter(partial_value.astype(jnp.bfloat16), 'head', scatter_dime...  73.1 us
    gather x16, local copies, waits for them, and re-layouts, attend_group(): low_blocks[block_ids].reshape(group_size, MAXB * BLOCK, 2, heads_here, HD)  44.2 us
    dot_general x8, matrix products, attend_group(): jnp.einsum('ghqk,gkhe->gqhe', weights, picked[:, :, 1], preferred_element...  32.6 us
    while x8, local copies, waits for them, and re-layouts  31.9 us
    all_to_all x1, waiting for transfers between devices, shards(): lax.all_to_all(view_qkv, 'tok', split_axis=0, concat_axis=0, tiled=True)  28.8 us
    dot_general x8, matrix products, attend_group(): jnp.einsum('gqhe,gkhe->ghqk', queries, picked[:, :, 0], preferred_element...  24.3 us
    reshape x1, local copies, waits for them, and re-layouts, shards(): per_view = arrived.reshape(VIEWS, -1, 3, heads_here, HD)  18.6 us
  transfers between devices with their start and end apart: 4, of which 3 were waited for; matrix products, arithmetic and copies ran while one was open for 33% of the time, Pallas kernels for 0%

commit v1 on v0

v1 whole, which is shorter than its diff:
```python
import functools
import math

import jax
import jax.numpy as jnp
from jax import lax
from jax.experimental import pallas as pl
from jax.experimental.pallas import tpu as pltpu
from jax.sharding import PartitionSpec as P

HD = 128
VIEWS = 8
BLOCK = 128
LOG2_SCALE = math.log2(math.e) / math.sqrt(HD)
VMEM_BYTES = 48 * 1024 * 1024
CONTRACT_LAST = (((1,), (1,)), ((), ()))


def rms_rows(row_block, norm_gain):
    values = row_block.astype(jnp.float32)
    factor = lax.rsqrt(jnp.mean(values * values, axis=-1, keepdims=True) + 1e-06)
    return (values * factor * norm_gain).astype(jnp.bfloat16)


def f32_dot(left, right):
    return jnp.dot(left, right, preferred_element_type=jnp.float32)


def block_diagonal(tiles):
    rows = []
    for index, tile in enumerate(tiles):
        zero = jnp.zeros_like(tile)
        rows.append(
            jnp.concatenate([tile if k == index else zero for k in range(len(tiles))], axis=1)
        )
    return jnp.concatenate(rows, axis=0)


def cross_kernel(
    lists_ref, counts_ref, tokens_ref, gain_ref, wq_ref, kv_ref, out_ref, vt_ref, q_ref
):
    step = pl.program_id(0)
    rows, cols = out_ref.shape
    heads = cols // HD
    low_rows = kv_ref.shape[0]
    per_step = rows // BLOCK
    listed = lists_ref.shape[1]

    @pl.when(step == 0)
    def _():
        def one_block(block, carry):
            start = pl.multiple_of(block * BLOCK, BLOCK)
            values = kv_ref[pl.ds(start, BLOCK), cols:]
            vt_ref[:, pl.ds(start, BLOCK)] = values.T
            return carry

        lax.fori_loop(0, low_rows // BLOCK, one_block, 0)

    normed = rms_rows(tokens_ref[...], gain_ref[...])
    q_ref[...] = (f32_dot(normed, wq_ref[...]) * LOG2_SCALE).astype(jnp.bfloat16)

    def one_block(local, carry):
        block = step * per_step + local
        row_start = pl.multiple_of(local * BLOCK, BLOCK)
        count = counts_ref[block]
        first = lists_ref[block, 0]
        starts = [
            pl.multiple_of(jnp.where(j < count, lists_ref[block, j], first) * BLOCK, BLOCK)
            for j in range(listed)
        ]
        query = block_diagonal(
            [q_ref[pl.ds(row_start, BLOCK), h * HD : (h + 1) * HD] for h in range(heads)]
        )
        keys = jnp.concatenate([kv_ref[pl.ds(s, BLOCK), :cols] for s in starts], axis=0)
        scores = lax.dot_general(keys, query, CONTRACT_LAST, preferred_element_type=jnp.float32)
        top = jnp.max(scores, axis=0, keepdims=True)
        weights = []
        total = jnp.zeros_like(top)
        for j in range(listed):
            shift = top + jnp.where(j < count, 0.0, 1e30)
            weight = jnp.exp2(scores[j * BLOCK : (j + 1) * BLOCK] - shift)
            total = total + jnp.sum(weight, axis=0, keepdims=True)
            weights.append(weight.astype(jnp.bfloat16))
        values_t = jnp.concatenate([vt_ref[:, pl.ds(s, BLOCK)] for s in starts], axis=1)
        mixed_t = f32_dot(values_t, jnp.concatenate(weights, axis=0)) / total
        for h in range(heads):
            part = slice(h * HD, (h + 1) * HD)
            out_ref[pl.ds(row_start, BLOCK), part] = mixed_t[part, part].T.astype(jnp.bfloat16)
        return carry

    lax.fori_loop(0, per_step, one_block, 0)


def cross_attention(hires_tokens, gain, w_cross_q, all_kv, block_lists, block_counts):
    tok_rows, width = hires_tokens.shape
    cols = w_cross_q.shape[1]
    low_rows = all_kv.shape[0]
    rows = math.gcd(tok_rows, 4 * BLOCK)
    return pl.pallas_call(
        cross_kernel,
        out_shape=jax.ShapeDtypeStruct((tok_rows, cols), jnp.bfloat16),
        grid_spec=pltpu.PrefetchScalarGridSpec(
            num_scalar_prefetch=2,
            grid=(tok_rows // rows,),
            in_specs=[
                pl.BlockSpec((rows, width), lambda i, *_: (i, 0)),
                pl.BlockSpec((1, width), lambda i, *_: (0, 0)),
                pl.BlockSpec((width, cols), lambda i, *_: (0, 0)),
                pl.BlockSpec((low_rows, 2 * cols), lambda i, *_: (0, 0)),
            ],
            out_specs=pl.BlockSpec((rows, cols), lambda i, *_: (i, 0)),
            scratch_shapes=[
                pltpu.VMEM((cols, low_rows), jnp.bfloat16),
                pltpu.VMEM((rows, cols), jnp.bfloat16),
            ],
        ),
        compiler_params=pltpu.CompilerParams(vmem_limit_bytes=VMEM_BYTES),
        cost_estimate=pl.CostEstimate(
            flops=2 * tok_rows * cols * (width + 2 * block_lists.shape[1] * BLOCK * 2),
            bytes_accessed=2 * tok_rows * (width + cols),
            transcendentals=tok_rows * block_lists.shape[1] * BLOCK * (cols // HD),
        ),
        name="cross",
    )(block_lists, block_counts, hires_tokens, gain, w_cross_q, all_kv)


def view_kernel(tokens_ref, gain_ref, w_ref, out_ref, qkv_ref, mixed_ref):
    _, sources, run, width = tokens_ref.shape
    cols = out_ref.shape[-1]
    heads = cols // HD
    rows = sources * run
    pixels = rows // VIEWS
    group = math.gcd(pixels, 32)
    gain = gain_ref[...]
    source_step = max(1, 256 // run)
    for s in range(0, sources, source_step):
        tokens = tokens_ref[0, s : s + source_step].reshape(source_step * run, width)
        projected = f32_dot(rms_rows(tokens, gain), w_ref[...])
        start = s * run
        stop = start + source_step * run
        qkv_ref[start:stop, :cols] = (projected[:, :cols] * LOG2_SCALE).astype(jnp.bfloat16)
        qkv_ref[start:stop, cols:] = projected[:, cols:].astype(jnp.bfloat16)
    size = VIEWS * group
    row_pixel = lax.broadcasted_iota(jnp.int32, (size, size), 0) % group
    col_pixel = lax.broadcasted_iota(jnp.int32, (size, size), 1) % group
    same = row_pixel == col_pixel

    def gathered(first, column):
        part = slice(column, column + HD)
        return jnp.concatenate(
            [qkv_ref[v * pixels + first : v * pixels + first + group, part] for v in range(VIEWS)],
            axis=0,
        )

    for first in range(0, pixels, group):
        for h in range(heads):
            query = gathered(first, h * HD)
            key = gathered(first, cols + h * HD)
            value = gathered(first, 2 * cols + h * HD)
            scores = lax.dot_general(query, key, CONTRACT_LAST, preferred_element_type=jnp.float32)
            scores = jnp.where(same, scores, -1e30)
            weight = jnp.exp2(scores - jnp.max(scores, axis=1, keepdims=True))
            total = jnp.sum(weight, axis=1, keepdims=True)
            mixed = (f32_dot(weight.astype(jnp.bfloat16), value) / total).astype(jnp.bfloat16)
            for v in range(VIEWS):
                mixed_ref[v * pixels + first : v * pixels + first + group, h * HD : (h + 1) * HD] = (
                    mixed[v * group : (v + 1) * group]
                )
    out_ref[:, 0] = mixed_ref[...].reshape(sources, run, cols)


def view_attention(tokens, gain, w_view):
    parts, sources, run, width = tokens.shape
    cols = w_view.shape[1] // 3
    rows = sources * run
    return pl.pallas_call(
        view_kernel,
        out_shape=jax.ShapeDtypeStruct((sources, parts, run, cols), jnp.bfloat16),
        grid=(parts,),
        in_specs=[
            pl.BlockSpec((1, sources, run, width), lambda i: (i, 0, 0, 0)),
            pl.BlockSpec((1, width), lambda i: (0, 0)),
            pl.BlockSpec((width, 3 * cols), lambda i: (0, 0)),
        ],
        out_specs=pl.BlockSpec((sources, 1, run, cols), lambda i: (0, i, 0, 0)),
        scratch_shapes=[
            pltpu.VMEM((rows, 3 * cols), jnp.bfloat16),
            pltpu.VMEM((rows, cols), jnp.bfloat16),
        ],
        compiler_params=pltpu.CompilerParams(vmem_limit_bytes=VMEM_BYTES),
        cost_estimate=pl.CostEstimate(
            flops=2 * parts * rows * cols * (3 * width + 512),
            bytes_accessed=2 * parts * rows * (width + cols),
            transcendentals=parts * rows * 512,
        ),
        name="view",
    )(tokens, gain, w_view)


def out_kernel(cross_ref, view_ref, w_ref, out_ref):
    total = f32_dot(cross_ref[...], w_ref[0]) + f32_dot(view_ref[...], w_ref[1])
    out_ref[...] = total.astype(jnp.bfloat16)


def out_projection(cross_out, view_out, w_out):
    tok_rows, cols = cross_out.shape
    width = w_out.shape[2]
    rows = math.gcd(tok_rows, 512)
    return pl.pallas_call(
        out_kernel,
        out_shape=jax.ShapeDtypeStruct((tok_rows, width), jnp.bfloat16),
        grid=(tok_rows // rows,),
        in_specs=[
            pl.BlockSpec((rows, cols), lambda i: (i, 0)),
            pl.BlockSpec((rows, cols), lambda i: (i, 0)),
            pl.BlockSpec((2, cols, width), lambda i: (0, 0, 0)),
        ],
        out_specs=pl.BlockSpec((rows, width), lambda i: (i, 0)),
        compiler_params=pltpu.CompilerParams(vmem_limit_bytes=VMEM_BYTES),
        cost_estimate=pl.CostEstimate(
            flops=4 * tok_rows * cols * width,
            bytes_accessed=2 * tok_rows * (2 * cols + width),
            transcendentals=0,
        ),
        name="project",
    )(cross_out, view_out, w_out)


def shards(
    n_head,
    n_tok,
    hires_tokens,
    lowres_tokens,
    norm_gain,
    w_cross_q,
    w_low_kv,
    w_view_qkv,
    w_out,
    block_lists,
    block_counts,
):
    tok_rows, width = hires_tokens.shape
    cols = w_cross_q.shape[1]
    run = tok_rows // (n_tok * n_head)
    head_index = lax.axis_index("head")
    gain = norm_gain.reshape(1, width)

    low_kv = f32_dot(
        rms_rows(lowres_tokens, norm_gain), w_low_kv.reshape(width, 2 * cols)
    ).astype(jnp.bfloat16)
    all_kv = lax.all_gather(low_kv, "tok", axis=0, tiled=True)

    to_send = lax.dynamic_index_in_dim(
        hires_tokens.reshape(n_tok, n_head, run, width), head_index, 1, keepdims=False
    )
    arrived = lax.all_to_all(to_send, "tok", split_axis=0, concat_axis=0, tiled=True)
    view_tokens = lax.all_gather(arrived, "head", axis=0, tiled=False)

    cross_out = cross_attention(hires_tokens, gain, w_cross_q, all_kv, block_lists, block_counts)
    mixed = view_attention(view_tokens, gain, w_view_qkv.reshape(width, 3 * cols))
    view_out = lax.all_to_all(
        mixed.reshape(tok_rows, cols), "tok", split_axis=0, concat_axis=0, tiled=True
    )
    partial_value = out_projection(cross_out, view_out, w_out)
    summed = lax.psum_scatter(
        partial_value, "head", scatter_dimension=1, tiled=True
    ).astype(jnp.float32)
    out_cols = summed.shape[1]
    residual = lax.dynamic_slice_in_dim(hires_tokens, head_index * out_cols, out_cols, 1)
    return (residual.astype(jnp.float32) + summed).astype(jnp.bfloat16)


def solution(mesh):
    in_specs = (
        P("tok", None),
        P("tok", None),
        P(),
        P(None, "head"),
        P(None, None, "head"),
        P(None, None, "head"),
        P(None, "head", None),
        P("tok", None),
        P("tok"),
    )
    out_specs = P("tok", "head")
    body = functools.partial(shards, mesh.shape["head"], mesh.shape["tok"])
    return jax.shard_map(body, mesh=mesh, in_specs=in_specs, out_specs=out_specs, check_vma=False)
```

time: 580 us -> 341 us (0.59)
  local copies, waits for them, and re-layouts: 170 us -> 11.7 us
  matrix products: 106 us -> 1.19 us
  waiting for transfers between devices: 265 us -> 186 us
  Pallas kernels: 0 us -> 63.2 us
  blocking collectives: 0 us -> 55.4 us
  starting transfers between devices: 12.2 us -> 5.72 us
  other arithmetic: 10.4 us -> 4.27 us
    dot_general x23 -> x1, matrix products: 106 us -> 1.19 us  [f32_dot(): return jnp.dot(left, right, preferred_element_type=jnp.float32)]
    all_gather x1, waiting for transfers between devices: 163 us -> 64.4 us  [shards(): all_kv = lax.all_gather(low_kv, 'tok', axis=0, tiled=True)]
    pallas_call x0 -> x3, Pallas kernels: none -> 63.2 us  [the longest x1 42 us: cross_attention(): pl.pallas_call(cross_kernel, out_shape=jax.ShapeDtypeStruct((tok_rows, co...]
    all_to_all x0 -> x1, blocking collectives: none -> 55.4 us  [shards(): lax.all_to_all(to_send, 'tok', split_axis=0, concat_axis=0, tiled=True)]
    all_gather x0 -> x1, waiting for transfers between devices: none -> 53 us  [shards(): view_tokens = lax.all_gather(arrived, 'head', axis=0, tiled=False)]
    gather x16 -> x0, local copies, waits for them, and re-layouts: 44.2 us -> none  [attend_group(): low_blocks[block_ids].reshape(group_size, MAXB * BLOCK, 2, heads_here, HD)]
    reshape x5 -> x1, local copies, waits for them, and re-layouts: 37.8 us -> 0.7 us  [shards(): w_view_qkv.reshape(width, 3 * cols)]
    while x8 -> x0, local copies, waits for them, and re-layouts: 31.9 us -> none
  transfers between devices with their start and end apart: 4 -> 4, of which waited for: 3 -> 3; matrix products, arithmetic and copies ran while one was open for 33% -> 1% of each run, Pallas kernels for 0% -> 16%
where the time goes in v1:
time: 341 us
  waiting for transfers between devices  186 us (55%)
  Pallas kernels  63.2 us (19%)
  blocking collectives  55.4 us (16%)
  between operations  13.2 us (4%)
  local copies, waits for them, and re-layouts  11.7 us (3%)
  starting transfers between devices  5.72 us (2%)
  other arithmetic  4.27 us (1%)
    reduce_scatter x1, waiting for transfers between devices, shards(): lax.psum_scatter(partial_value, 'head', scatter_dimension=1, tiled=True)  68.6 us
    all_gather x1, waiting for transfers between devices, shards(): all_kv = lax.all_gather(low_kv, 'tok', axis=0, tiled=True)  64.4 us
    all_to_all x1, blocking collectives, shards(): lax.all_to_all(to_send, 'tok', split_axis=0, concat_axis=0, tiled=True)  55.4 us
    all_gather x1, waiting for transfers between devices, shards(): view_tokens = lax.all_gather(arrived, 'head', axis=0, tiled=False)  53 us
    pallas_call x1, Pallas kernels, cross_attention(): pl.pallas_call(cross_kernel, out_shape=jax.ShapeDtypeStruct((tok_rows, co...  42 us
    pallas_call x1, Pallas kernels, view_attention(): pl.pallas_call(view_kernel, out_shape=jax.ShapeDtypeStruct((sources, part...  13.7 us
    unnamed x27, local copies, waits for them, and re-layouts  9.22 us
    pallas_call x1, Pallas kernels, out_projection(): pl.pallas_call(out_kernel, out_shape=jax.ShapeDtypeStruct((tok_rows, widt...  7.63 us
  transfers between devices with their start and end apart: 4, of which 3 were waited for; matrix products, arithmetic and copies ran while one was open for 1% of the time, Pallas kernels for 16%

profile of v1, /device:TPU:0, one launch (start us, length us, event | category | flops | bytes accessed | tf_op | source)
XLA Modules:
  0.0 340.8 jit_solution(2097478131035120986)
XLA Ops:
  6.5 0.0 all-gather.6.cloned.1.call-start
  6.5 1.8 dynamic-slice_bitcast_fusion
  8.3 55.4 %all_to_all.16 = bf16[8,128,1024]{2,1,0:T(8,128)(2,1)} all-to-all(bf16[8,128,1024]{2,1,0:T(8,128)(2,1)S(1)} %dynamic-slice_bitcast_fusion), channel_id=1, replica_groups=mesh['head'=4,'tok'=8] {'tok'}, dimensions={0} | all-to-all | bytes 4194304 | tf_op jit(solution)/shard_map/all_to_all | solution.py:256
  63.7 0.0 copy-start.9
  63.7 0.0 copy-start.10
  63.7 0.0 copy-start.4
  63.7 0.0 all-gather.6.cloned.1.call-update
  63.7 0.0 all-gather.4.cloned.1.call-start
  63.8 1.1 copy-done.9
  64.9 0.0 copy-start.8
  64.9 0.2 copy.20
  65.2 0.0 copy-done.10
  65.2 0.2 fusion
  65.4 0.0 copy-done.4
  65.4 1.2 convolution_convert_fusion
  66.6 0.0 all-gather.4.cloned.1.call-update
  66.6 0.0 copy-done.8
  66.6 0.9 copy.17
  67.5 0.7 copy.18.w_ref
  68.2 53.0 %all-gather.6.cloned.1.call-done = bf16[32,128,1024]{2,1,0:T(8,128)(2,1)} async-done(((bf16[8,128,1024]{2,1,0:T(8,128)(2,1)}), bf16[32,128,1024]{2,1,0:T(8,128)(2,1)}) %all-gather.6.cloned.1.call-update) | async-done | bytes 8388624 | tf_op jit(solution)/shard_map/all_gather | solution.py:257
  121.2 13.7 %view.1 = bf16[8,4,128,256]{3,2,1,0:T(8,128)(2,1)S(1)} custom-call(bf16[4,8,128,1024]{3,2,1,0:T(8,128)(2,1)} %bitcast.21, f32[1,1024]{1,0:T(1,128)S(1)} %bitcast.15, bf16[1024,768]{1,0:T(8,128)(2,1)S(1)} %copy.18.w_ref), custom_call_target="tpu_custom_call" | custom-call | flops 7516192768 | bytes 10485760 | tf_op jit(solution)/shard_map/view/pallas_call | solution.py:176
  134.9 0.0 copy-start
  134.9 1.3 copy-done
  136.2 0.0 copy-start.11
  136.2 0.0 copy-start.5
  136.2 5.6 %all-to-all-start.1 = ((bf16[8,512,256]{2,1,0:T(8,128)(2,1)}), bf16[8,512,256]{2,1,0:T(8,128)(2,1)S(1)}, u32[]{:S(2)}, u32[]{:S(2)}) async-start(bf16[8,512,256]{2,1,0:T(8,128)(2,1)} %bitcast.14), calls=%async_computation.1 | async-start | bytes 4194304 | tf_op jit(solution)/shard_map/all_to_all | solution.py:261
  141.9 0.0 reduce-scatter.2.cloned.1.call-start
  141.9 0.0 copy-done.11
  141.9 0.1 copy.15.lists_ref
  142.0 64.4 %all-gather.4.cloned.1.call-done.kv_ref = bf16[2048,512]{1,0:T(8,128)(2,1)} async-done(((bf16[256,512]{1,0:T(8,128)(2,1)}), bf16[2048,512]{1,0:T(8,128)(2,1)}) %all-gather.4.cloned.1.call-update) | async-done | bytes 2097168 | tf_op jit(solution)/shard_map/all_gather | solution.py:251
  206.4 0.0 copy-done.5
  206.4 0.0 copy-start.1
  206.4 1.6 copy-done.1
  208.0 0.0 copy-start.3
  208.0 1.0 copy-done.3
  209.0 0.0 copy-start.2
  209.0 42.0 %cross.1.cross_ref = bf16[4096,256]{1,0:T(8,128)(2,1)S(1)} custom-call(s32[32,8]{1,0:T(8,128)S(1)} %copy.15.lists_ref, s32[32]{0:T(128)S(1)} %copy-done.5, bf16[4096,1024]{1,0:T(8,128)(2,1)} %tokens_ref.1, f32[1,1024]{1,0:T(1,128)S(1)} %bitcast.16, bf16[1024,256]{1,0:T(8,128)(2,1)S(1)} %copy-done.3, bf16[2048,512]{1,0:T(8,128)(2,1)S(1)} %copy-done.1), custom_call_target="tpu_custom_call" | custom-call | flops 10737418240 | bytes 10485760 | tf_op jit(solution)/shard_map/cross/pallas_call | solution.py:99
  251.0 0.0 copy-start.6
  251.0 1.3 copy-done.6
  252.3 0.0 all-to-all-done.1
  252.3 0.0 copy-done.2
  252.3 0.0 copy-start.7
  252.3 1.6 copy-done.7
  253.9 7.6 %project.1 = bf16[4096,1024]{1,0:T(8,128)(2,1)} custom-call(bf16[4096,256]{1,0:T(8,128)(2,1)S(1)} %copy-done.7, bf16[4096,256]{1,0:T(8,128)(2,1)S(1)} %bitcast.13, bf16[2,256,1024]{2,1,0:T(8,128)(2,1)S(1)} %copy-done.2), custom_call_target="tpu_custom_call" | custom-call | flops 4294967296 | bytes 12582912 | tf_op jit(solution)/shard_map/project/pallas_call | solution.py:209
  261.5 0.0 reduce-scatter.2.cloned.1.call-update
  261.6 68.6 %reduce-scatter.2.cloned.1.call-done = bf16[4096,256]{1,0:T(8,128)(2,1)} async-done(((bf16[4096,1024]{1,0:T(8,128)(2,1)}), bf16[4096,256]{1,0:T(8,128)(2,1)}) %reduce-scatter.2.cloned.1.call-update) | async-done | bytes 2097168 | tf_op jit(solution)/shard_map/reduce_scatter | solution.py:265
  330.2 4.1 %add_convert_fusion = bf16[4096,256]{1,0:T(8,128)(2,1)} fusion(bf16[4096,256]{1,0:T(8,128)(2,1)} %reduce-scatter.2.cloned.1.call-done, bf16[4096,1024]{1,0:T(8,128)(2,1)} %tokens_ref.1, s32[]{:T(128)S(6)} %select_n.7), kind=kLoop, calls=%fused_computation | loop fusion | flops 4194304 | bytes 6291460 | tf_op jit(solution)/shard_map/convert_element_type | solution.py:270
  (1 shorter events, 0.0 us)
Async XLA Ops:
  6.5 114.7 %all-gather.6.cloned.1.call-start = ((), (), s32[]{:S(2)}) async-start(), calls=%async_computation.5 | async-start | bytes 10485760 | tf_op jit(solution)/shard_map/all_gather | solution.py:257
  63.7 1.2 copy-start.9
  63.7 1.5 copy-start.10
  63.7 1.7 copy-start.4
  63.7 142.6 %all-gather.4.cloned.1.call-start = ((), (), s32[]{:S(2)}) async-start(), calls=%async_computation.3 | async-start | bytes 2359296 | tf_op jit(solution)/shard_map/all_gather | solution.py:251
  64.9 1.7 copy-start.8
  134.9 1.3 copy-start
  136.2 5.7 %copy-start.11 = (s32[32,8]{0,1:T(8,128)S(1)}, s32[32,8]{0,1:T(8,128)}, u32[]{:S(2)}) copy-start(s32[32,8]{0,1:T(8,128)} %param.16) | copy-start | bytes 3076
  136.2 70.2 %copy-start.5 = (s32[32]{0:T(128)S(1)}, s32[32]{0:T(128)}, u32[]{:S(2)}) copy-start(s32[32]{0:T(128)} %counts_ref.1) | copy-start | bytes 388
  136.2 116.1 %all-to-all-start.1 = ((bf16[8,512,256]{2,1,0:T(8,128)(2,1)}), bf16[8,512,256]{2,1,0:T(8,128)(2,1)S(1)}, u32[]{:S(2)}, u32[]{:S(2)}) async-start(bf16[8,512,256]{2,1,0:T(8,128)(2,1)} %bitcast.14), calls=%async_computation.1 | async-start | bytes 4194304 | tf_op jit(solution)/shard_map/all_to_all | solution.py:261
  141.9 188.3 %reduce-scatter.2.cloned.1.call-start = ((), (), s32[]{:S(2)}) async-start(), calls=%async_computation.4 | async-start | bytes 10485760 | tf_op jit(solution)/shard_map/reduce_scatter | solution.py:265
  206.4 1.6 copy-start.1
  208.0 1.0 copy-start.3
  209.0 43.3 %copy-start.2 = (bf16[2,256,1024]{2,1,0:T(8,128)(2,1)S(1)}, bf16[2,256,1024]{2,1,0:T(8,128)(2,1)}, u32[]{:S(2)}) copy-start(bf16[2,256,1024]{2,1,0:T(8,128)(2,1)} %w_ref.1) | copy-start | bytes 3145732
  251.0 1.3 copy-start.6
  252.3 1.6 copy-start.7
Sparse Core Ops, SparseCore 0:
  63.9 57.3 all-gather.5
  123.3 82.9 all-gather.3
  261.7 68.4 reduce-scatter.1
